TPU v7x, 256 devices: a whole 4x4x8 slice. The times are simulated.
256 devices in a mesh: qa: 8 (over y_lo, x), qb: 32 (over y_hi, z, core).
Axes of the slice: x: 4, y: 4 (y_hi: 2, y_lo: 2; y = y_hi * 2 + y_lo), z: 8, core: 2. Of those that a mesh axis runs over, the one named last changes fastest.
Arguments:
- amplitudes: float32 [2, 16777216], P(None, ('qa', 'qb')), may hold values from -6 to 6
- gate_blocks: float32 [4, 6, 2, 128, 128], replicated, may hold values from -0.375 to 0.375
- phase_low: float32 [4, 256], replicated, may hold values from -3.140625 to 3.140625
- phase_high: float32 [4, 256], replicated, may hold values from -3.140625 to 3.140625
- phase_global: float32 [4, 8, 32], P(None, 'qa', 'qb'), may hold values from -3.140625 to 3.140625
Outputs:
- final_state: float32 [2, 16777216], P(None, ('qa', 'qb'))
All inputs are finite; a program needn't handle non-finite values.
Results may differ from a plain program's by a relative error of at most 0.00011.
Values sent between devices are 32-bit elements; how exact they have to be, the bound alone decides.
A program may use at most 64 MiB of HBM per device.

v0:
```python
import jax
import jax.numpy as jnp
from jax import lax
from jax.sharding import PartitionSpec as P


def apply_gate(state, matrix, where):
    width = matrix.shape[-1]
    cells = state.shape[2]
    stacked = jnp.concatenate([matrix[0], matrix[1]], axis=0)
    if where == 0:
        values = state.reshape(2 * (cells // width), width)
        product = lax.dot_general(
            values, stacked, (((1,), (1,)), ((), ())), precision=lax.Precision.HIGHEST
        )
        product = product.reshape(2, cells // width, 2, width)
        out_real = product[0, :, 0] - product[1, :, 1]
        out_imag = product[0, :, 1] + product[1, :, 0]
    elif where == 1:
        upper = cells // (width * width)
        values = state.reshape(2, upper, width, width)
        product = lax.dot_general(
            stacked, values, (((1,), (2,)), ((), ())), precision=lax.Precision.HIGHEST
        )
        product = product.reshape(2, width, 2, upper, width)
        out_real = jnp.transpose(product[0, :, 0] - product[1, :, 1], (1, 0, 2))
        out_imag = jnp.transpose(product[1, :, 0] + product[0, :, 1], (1, 0, 2))
    else:
        values = state.reshape(2, width, cells // width)
        product = lax.dot_general(
            stacked, values, (((1,), (1,)), ((), ())), precision=lax.Precision.HIGHEST
        )
        product = product.reshape(2, width, 2, cells // width)
        out_real = product[0, :, 0] - product[1, :, 1]
        out_imag = product[1, :, 0] + product[0, :, 1]
    return jnp.stack([out_real.reshape(cells), out_imag.reshape(cells)]).reshape(2, 1, cells)


def apply_phase(state, low_angles, high_angles, global_angles):
    local = (high_angles[:, None] + low_angles[None, :]).reshape(-1)
    theta = global_angles.reshape(-1, 1) + local[None, :]
    cosine = jnp.cos(theta)
    sine = jnp.sin(theta)
    return jnp.stack([state[0] * cosine - state[1] * sine, state[0] * sine + state[1] * cosine])


def regroup_with_gate(state, which, matrix):
    cells = state.shape[2]
    width = matrix.shape[-1]

    def lowest_gate(pieces):
        shape = pieces.shape
        flat = pieces.reshape(2, 1, shape[1] * shape[2] * shape[3])
        return apply_gate(flat, matrix, 0).reshape(shape)

    if which == 0:
        count = lax.axis_size("qa")
        blocks = state.reshape(2, count, cells // (count * width), width)
        moved = lowest_gate(lax.all_to_all(blocks, "qa", split_axis=1, concat_axis=1, tiled=True))
    else:
        count = lax.axis_size("qb")
        blocks = state.reshape(2, count, cells // (count * width), width)
        moved = lowest_gate(lax.all_to_all(blocks, "qb", split_axis=1, concat_axis=1, tiled=True))
    return moved.reshape(2, 1, cells)


def body(amplitudes, gate_blocks, phase_low, phase_high, phase_global):
    cells = amplitudes.shape[1]
    state = amplitudes.reshape(2, 1, cells)
    segments = gate_blocks.shape[0]
    per_segment = gate_blocks.shape[1]
    done_lowest = False
    for segment in range(segments):
        for gate in range(per_segment):
            if gate == 0 and done_lowest:
                continue
            state = apply_gate(state, gate_blocks[segment, gate], gate % 3)
        done_lowest = False
        state = apply_phase(
            state, phase_low[segment], phase_high[segment], phase_global[segment].reshape(1)
        )
        if segment < 3:
            which = 1 if segment == 1 else 0
            state = regroup_with_gate(state, which, gate_blocks[segment + 1, 0])
            done_lowest = True
    return state.reshape(2, cells)


def solution(mesh):
    return jax.shard_map(
        body,
        mesh=mesh,
        in_specs=(P(None, ("qa", "qb")), P(), P(), P(), P(None, "qa", "qb")),
        out_specs=P(None, ("qa", "qb")),
        check_vma=False,
    )
```

profile of v0, /device:TPU:32, one launch (start us, length us, event | category | flops | bytes accessed | tf_op | source)
XLA Modules:
  0.0 105.7 jit_solution(10410167867592833478)
XLA Ops:
  0.0 2.2 %slice_bitcast_fusion.3 = (f32[128,128]{1,0:T(8,128)S(1)}, f32[128,128]{1,0:T(8,128)S(1)}, f32[128,128]{1,0:T(8,128)S(1)}, f32[128,128]{1,0:T(8,128)S(1)}, f32[1...) fusion(f32[4,6,2,128,128]{4,3,2,1,0:T(8,128)} %param.6), kind=kLoop, calls=%fused_computation.214 | loop fusion | bytes 2490368 | tf_op jit(solution)/shard_map/squeeze | solution.py:10
  2.2 2.1 %slice_bitcast_fusion.21 = (f32[128,128]{1,0:T(8,128)}, f32[128,128]{1,0:T(8,128)}, f32[128,128]{1,0:T(8,128)}, f32[128,128]{1,0:T(8,128)S(1)}, f32[128,128]{1,0...) fusion(f32[4,6,2,128,128]{4,3,2,1,0:T(8,128)} %param.6), kind=kLoop, calls=%fused_computation.232 | loop fusion | bytes 2490368 | tf_op jit(solution)/shard_map/squeeze | solution.py:10
  4.3 0.5 reshape_reshape.2
  4.8 1.9 %convolution_bitcast_fusion = f32[1024,256]{0,1:T(8,128)S(1)} fusion(f32[1024,128]{1,0:T(8,128)S(1)} %reshape_reshape.2, f32[128,128]{1,0:T(8,128)} %get-tuple-element.20, f32[128,128]{1,0:T(8,128)} %get-tuple-element.21), kind=kOutput, calls=%fused_computation | convolution fusion | flops 402685952 | bytes 1703936 | tf_op jit(solution)/shard_map/dot_general | solution.py:13
  6.6 0.9 reshape.1369
  7.5 0.5 slice_subtract_fusion.23
  8.4 1.0 pad_maximum_fusion.17
  9.3 1.0 fusion
  10.5 1.0 fusion.3
  11.8 1.0 fusion.6
  12.9 1.0 fusion.9
  14.1 1.0 fusion.12
  15.5 0.7 fusion.117
  16.2 1.8 %fusion.82 = (f32[1,8,64,128]{3,2,0,1:T(8,128)S(1)}, f32[1,8,64,128]{3,2,0,1:T(8,128)S(1)}) fusion(f32[1,8,64,128]{3,2,1,0:T(8,128)S(1)} %add.638, f32[1,8,64,128]{3,2,1,0:T(8,128)S(1)} %sub.368, f32[64,128]{1,0:T(8,128)S(1)} %bitcast.579, f32[8,64]{1,0:T(8,128)S(1)} %copy.27, f32[]{:T(128)} %bitcast.106), kind=kLoop, calls=%fused_computation.169 | loop fusion | flops 524288 | bytes 1083396 | tf_op jit(solution)/shard_map/sub | solution.py:44
  18.0 0.8 pad_maximum_fusion
  18.9 5.3 %all-to-all-start = ((f32[2,8,64,128]{3,2,0,1:T(8,128)}), f32[2,8,64,128]{3,2,0,1:T(8,128)S(1)}, u32[]{:S(2)}, u32[]{:S(2)}) async-start(f32[2,8,64,128]{3,2,0,1:T(8,128)} %pad_maximum_fusion), calls=%async_computation | async-start | bytes 1048576 | tf_op jit(solution)/shard_map/all_to_all | solution.py:59
  24.5 9.7 %all-to-all-done = f32[2,8,64,128]{3,2,0,1:T(8,128)S(1)} async-done(((f32[2,8,64,128]{3,2,0,1:T(8,128)}), f32[2,8,64,128]{3,2,0,1:T(8,128)S(1)}, u32[]{:S(2)}, u32[]{:S(2)}) %all-to-all-start) | async-done | bytes 524320 | tf_op jit(solution)/shard_map/all_to_all | solution.py:59
  34.3 1.0 fusion.118
  35.4 1.0 fusion.15
  36.5 1.0 fusion.18
  37.7 1.0 fusion.21
  38.7 1.0 fusion.24
  39.9 1.0 fusion.27
  41.0 1.7 %fusion.80 = (f32[1,32,16,128]{3,2,0,1:T(8,128)S(1)}, f32[1,32,16,128]{3,2,0,1:T(8,128)S(1)}) fusion(f32[1,32,16,128]{3,2,1,0:T(8,128)S(1)} %add.663, f32[1,32,16,128]{3,2,1,0:T(8,128)S(1)} %sub.381, f32[16,128]{1,0:T(8,128)S(1)} %bitcast.582, f32[32,16]{1,0:T(8,128)S(1)} %copy.34, f32[]{:T(128)} %bitcast.143), kind=kLoop, calls=%fused_computation.163 | loop fusion | flops 524288 | bytes 1058820 | tf_op jit(solution)/shard_map/sub | solution.py:44
  42.8 0.8 pad_maximum_fusion.1
  43.6 11.1 %all-to-all-start.1 = ((f32[2,32,16,128]{3,2,0,1:T(8,128)}), f32[2,32,16,128]{3,2,0,1:T(8,128)S(1)}, u32[]{:S(2)}, u32[]{:S(2)}) async-start(f32[2,32,16,128]{3,2,0,1:T(8,128)} %pad_maximum_fusion.1), calls=%async_computation.1 | async-start | bytes 1048576 | tf_op jit(solution)/shard_map/all_to_all | solution.py:63
  54.9 1.6 %fusion.84 = (f32[256,256]{1,0:T(8,128)S(1)}, f32[256,256]{1,0:T(8,128)S(1)}) fusion(f32[256]{0:T(256)S(1)} %bitcast.585, f32[256]{0:T(256)S(1)} %bitcast.584, f32[]{:T(128)} %bitcast.217), kind=kLoop, calls=%fused_computation.174 | loop fusion | flops 131072 | bytes 526340 | tf_op jit(solution)/shard_map/sin | solution.py:43
  57.2 1.2 %slice_bitcast_fusion.41 = (f32[128,128]{1,0:T(8,128)S(1)}, f32[128,128]{1,0:T(8,128)S(1)}, f32[128,128]{1,0:T(8,128)S(1)}, f32[128,128]{1,0:T(8,128)S(1)}, f32[...) fusion(f32[4,6,2,128,128]{4,3,2,1,0:T(8,128)} %param.6), kind=kLoop, calls=%fused_computation.252 | loop fusion | bytes 1310720 | tf_op jit(solution)/shard_map/squeeze | solution.py:10
  58.3 15.6 %all-to-all-done.1 = f32[2,32,16,128]{3,2,0,1:T(8,128)S(1)} async-done(((f32[2,32,16,128]{3,2,0,1:T(8,128)}), f32[2,32,16,128]{3,2,0,1:T(8,128)S(1)}, u32[]{:S(2)}, u32[]{:S(2)}) %all-to-all-start.1) | async-done | bytes 524320 | tf_op jit(solution)/shard_map/all_to_all | solution.py:63
  73.9 1.0 fusion.119
  75.0 1.0 fusion.30
  76.2 1.0 fusion.33
  77.3 1.0 fusion.36
  78.3 1.0 fusion.39
  79.5 1.0 fusion.42
  80.6 1.9 %fusion.78 = (f32[1,8,64,128]{3,2,0,1:T(8,128)S(1)}, f32[1,8,64,128]{3,2,0,1:T(8,128)S(1)}) fusion(f32[1,8,64,128]{3,2,1,0:T(8,128)S(1)} %add.688, f32[1,8,64,128]{3,2,1,0:T(8,128)S(1)} %sub.394, f32[64,128]{1,0:T(8,128)S(1)} %bitcast.578, f32[8,64]{1,0:T(8,128)S(1)} %copy.41, f32[]{:T(128)} %bitcast.180), kind=kLoop, calls=%fused_computation.157 | loop fusion | flops 524288 | bytes 1083396 | tf_op jit(solution)/shard_map/sub | solution.py:44
  82.5 0.8 pad_maximum_fusion.2
  83.3 3.8 %all-to-all-start.2 = ((f32[2,8,64,128]{3,2,0,1:T(8,128)}), f32[2,8,64,128]{3,2,0,1:T(8,128)S(1)}, u32[]{:S(2)}, u32[]{:S(2)}) async-start(f32[2,8,64,128]{3,2,0,1:T(8,128)} %pad_maximum_fusion.2), calls=%async_computation.2 | async-start | bytes 1048576 | tf_op jit(solution)/shard_map/all_to_all | solution.py:59
  87.2 9.3 %all-to-all-done.2 = f32[2,8,64,128]{3,2,0,1:T(8,128)S(1)} async-done(((f32[2,8,64,128]{3,2,0,1:T(8,128)}), f32[2,8,64,128]{3,2,0,1:T(8,128)S(1)}, u32[]{:S(2)}, u32[]{:S(2)}) %all-to-all-start.2) | async-done | bytes 524320 | tf_op jit(solution)/shard_map/all_to_all | solution.py:59
  96.6 1.0 fusion.120
  97.6 1.0 fusion.45
  98.8 1.0 fusion.48
  99.9 1.0 fusion.51
  101.0 1.0 fusion.54
  102.1 1.0 fusion.57
  103.2 0.3 add.709
  103.8 0.5 fusion.76
  104.4 1.3 %maximum_bitcast_fusion.40 = f32[2,65536]{1,0:T(2,128)} fusion(f32[1,1,65536]{2,0,1:T(1,128)S(1)} %get-tuple-element.57, f32[1,1,65536]{2,0,1:T(1,128)S(1)} %get-tuple-element.56), kind=kLoop, calls=%fused_computation.84 | loop fusion | flops 131072 | bytes 1048576 | tf_op jit(solution)/shard_map/reshape | solution.py:86
  (119 shorter events, 4.7 us)
Async XLA Ops:
  0.0 4.3 %copy-start = (f32[2,65536]{1,0:T(2,128)S(1)}, f32[2,65536]{1,0:T(2,128)}, u32[]{:S(2)}) copy-start(f32[2,65536]{1,0:T(2,128)} %param.5) | copy-start | bytes 1572868
  10.3 1.4 %copy-start.7 = (f32[128,128]{1,0:T(8,128)S(1)}, f32[128,128]{1,0:T(8,128)}, u32[]{:S(2)}) copy-start(f32[128,128]{1,0:T(8,128)} %get-tuple-element.14) | copy-start | bytes 196612
  10.3 1.4 %copy-start.8 = (f32[128,128]{1,0:T(8,128)S(1)}, f32[128,128]{1,0:T(8,128)}, u32[]{:S(2)}) copy-start(f32[128,128]{1,0:T(8,128)} %get-tuple-element.15) | copy-start | bytes 196612
  10.3 1.4 %copy-start.9 = (f32[128,128]{1,0:T(8,128)S(1)}, f32[128,128]{1,0:T(8,128)}, u32[]{:S(2)}) copy-start(f32[128,128]{1,0:T(8,128)} %get-tuple-element.18) | copy-start | bytes 196612
  10.4 1.4 %copy-start.10 = (f32[128,128]{1,0:T(8,128)S(1)}, f32[128,128]{1,0:T(8,128)}, u32[]{:S(2)}) copy-start(f32[128,128]{1,0:T(8,128)} %get-tuple-element.19) | copy-start | bytes 196612
  11.5 1.3 %copy-start.3 = (f32[128,128]{1,0:T(8,128)S(1)}, f32[128,128]{1,0:T(8,128)}, u32[]{:S(2)}) copy-start(f32[128,128]{1,0:T(8,128)} %get-tuple-element.26) | copy-start | bytes 196612
  11.5 1.3 %copy-start.4 = (f32[128,128]{1,0:T(8,128)S(1)}, f32[128,128]{1,0:T(8,128)}, u32[]{:S(2)}) copy-start(f32[128,128]{1,0:T(8,128)} %get-tuple-element.27) | copy-start | bytes 196612
  11.5 1.3 %copy-start.5 = (f32[128,128]{1,0:T(8,128)S(1)}, f32[128,128]{1,0:T(8,128)}, u32[]{:S(2)}) copy-start(f32[128,128]{1,0:T(8,128)} %get-tuple-element.28) | copy-start | bytes 196612
  11.5 1.3 %copy-start.6 = (f32[128,128]{1,0:T(8,128)S(1)}, f32[128,128]{1,0:T(8,128)}, u32[]{:S(2)}) copy-start(f32[128,128]{1,0:T(8,128)} %get-tuple-element.29) | copy-start | bytes 196612
  13.9 1.4 %copy-start.12 = (f32[4,256]{1,0:T(4,128)S(1)}, f32[4,256]{1,0:T(4,128)}, u32[]{:S(2)}) copy-start(f32[4,256]{1,0:T(4,128)} %param.8) | copy-start | bytes 12292
  14.0 1.5 %copy-start.13 = (f32[4,256]{1,0:T(4,128)S(1)}, f32[4,256]{1,0:T(4,128)}, u32[]{:S(2)}) copy-start(f32[4,256]{1,0:T(4,128)} %param.7) | copy-start | bytes 12292
  14.0 1.5 %copy-start.11 = (f32[4,1,1]{0,2,1:T(1,128)S(1)}, f32[4,1,1]{0,2,1:T(1,128)}, u32[]{:S(2)}) copy-start(f32[4,1,1]{0,2,1:T(1,128)} %param.9) | copy-start | bytes 52
  15.1 9.4 %copy-start.1 = (f32[128,128]{1,0:T(8,128)S(1)}, f32[128,128]{1,0:T(8,128)}, u32[]{:S(2)}) copy-start(f32[128,128]{1,0:T(8,128)} %get-tuple-element.32) | copy-start | bytes 196612
  15.1 9.4 %copy-start.2 = (f32[128,128]{1,0:T(8,128)S(1)}, f32[128,128]{1,0:T(8,128)}, u32[]{:S(2)}) copy-start(f32[128,128]{1,0:T(8,128)} %get-tuple-element.33) | copy-start | bytes 196612
  18.9 15.4 %all-to-all-start = ((f32[2,8,64,128]{3,2,0,1:T(8,128)}), f32[2,8,64,128]{3,2,0,1:T(8,128)S(1)}, u32[]{:S(2)}, u32[]{:S(2)}) async-start(f32[2,8,64,128]{3,2,0,1:T(8,128)} %pad_maximum_fusion), calls=%async_computation | async-start | bytes 1048576 | tf_op jit(solution)/shard_map/all_to_all | solution.py:59
  43.6 30.3 %all-to-all-start.1 = ((f32[2,32,16,128]{3,2,0,1:T(8,128)}), f32[2,32,16,128]{3,2,0,1:T(8,128)S(1)}, u32[]{:S(2)}, u32[]{:S(2)}) async-start(f32[2,32,16,128]{3,2,0,1:T(8,128)} %pad_maximum_fusion.1), calls=%async_computation.1 | async-start | bytes 1048576 | tf_op jit(solution)/shard_map/all_to_all | solution.py:63
  83.3 13.2 %all-to-all-start.2 = ((f32[2,8,64,128]{3,2,0,1:T(8,128)}), f32[2,8,64,128]{3,2,0,1:T(8,128)S(1)}, u32[]{:S(2)}, u32[]{:S(2)}) async-start(f32[2,8,64,128]{3,2,0,1:T(8,128)} %pad_maximum_fusion.2), calls=%async_computation.2 | async-start | bytes 1048576 | tf_op jit(solution)/shard_map/all_to_all | solution.py:59
where the time goes:
time: 106 us
  waiting for transfers between devices  34.6 us (33%)
  matrix products  24.5 us (23%)
  starting transfers between devices  20.1 us (19%)
  other arithmetic  14.6 us (14%)
  local copies, waits for them, and re-layouts  10.7 us (10%)
  between operations  1.1 us (1%)
    all_to_all x2, waiting for transfers between devices, regroup_with_gate(): lax.all_to_all(blocks, 'qa', split_axis=1, concat_axis=1, tiled=True)  19.1 us
    all_to_all x1, waiting for transfers between devices, regroup_with_gate(): lax.all_to_all(blocks, 'qb', split_axis=1, concat_axis=1, tiled=True)  15.6 us
    all_to_all x1, starting transfers between devices, regroup_with_gate(): lax.all_to_all(blocks, 'qb', split_axis=1, concat_axis=1, tiled=True)  11.1 us
    all_to_all x2, starting transfers between devices, regroup_with_gate(): lax.all_to_all(blocks, 'qa', split_axis=1, concat_axis=1, tiled=True)  9.08 us
    dot_general x8, matrix products, apply_gate(): lax.dot_general(values, stacked, (((1,), (1,)), ((), ())), precision=lax....  8.76 us
    dot_general x8, matrix products, apply_gate(): lax.dot_general(stacked, values, (((1,), (1,)), ((), ())), precision=lax....  7.85 us
    dot_general x8, matrix products, apply_gate(): lax.dot_general(stacked, values, (((1,), (2,)), ((), ())), precision=lax....  7.84 us
    sub x4, other arithmetic, apply_phase(): state[0] * cosine - state[1] * sine  5.93 us
  transfers between devices with their start and end apart: 3, of which 3 were waited for; matrix products, arithmetic and copies ran while one was open for 4% of the time, Pallas kernels for 0%

commit v1 on v0

--- a/solution.py
+++ b/solution.py
@@ -56,7 +56,14 @@
     if which == 0:
         count = lax.axis_size("qa")
         blocks = state.reshape(2, count, cells // (count * width), width)
-        moved = lowest_gate(lax.all_to_all(blocks, "qa", split_axis=1, concat_axis=1, tiled=True))
+        moved = lowest_gate(
+            jnp.concatenate(
+                lax.all_to_all(
+                    jnp.stack(jnp.split(blocks, lax.axis_size("qa"), axis=1)), "qa", 0, 0
+                ),
+                axis=1,
+            )
+        )
     else:
         count = lax.axis_size("qb")
         blocks = state.reshape(2, count, cells // (count * width), width)

time: 106 us -> 115 us (1.085)
  other arithmetic: 14.6 us -> 23 us
    unnamed x0 -> x14, other arithmetic: none -> 8.87 us
    add x0 -> x2, other arithmetic: none -> 3.67 us  [apply_phase(): state[0] * sine + state[1] * cosine]
    sub x4 -> x2, other arithmetic: 5.93 us -> 2.26 us  [apply_phase(): state[0] * cosine - state[1] * sine]
    another operation x3 -> x1, other arithmetic: 2.5 us -> 0.83 us  [apply_phase(): jnp.stack([state[0] * cosine - state[1] * sine, state[0] * sine + state[1...]
    another operation x0 -> x2, other arithmetic: none -> 1.27 us  [regroup_with_gate(): jnp.stack(jnp.split(blocks, lax.axis_size('qa'), axis=1))]
  transfers between devices with their start and end apart: 3 -> 3, of which waited for: 3 -> 3; matrix products, arithmetic and copies ran while one was open for 4% -> 3% of each run, Pallas kernels for 0% -> 0%
where the time goes in v1:
time: 115 us; the launch traced here: 114 us
  waiting for transfers between devices  34.7 us (30%)
  matrix products  24.5 us (21%)
  other arithmetic  23 us (20%)
  starting transfers between devices  20.1 us (17%)
  local copies, waits for them, and re-layouts  10.7 us (9%)
    all_to_all x2, waiting for transfers between devices, regroup_with_gate(): lax.all_to_all(jnp.stack(jnp.split(blocks, lax.axis_size('qa'), axis=1)),...  19.1 us
    all_to_all x1, waiting for transfers between devices, regroup_with_gate(): lax.all_to_all(blocks, 'qb', split_axis=1, concat_axis=1, tiled=True)  15.6 us
    all_to_all x1, starting transfers between devices, regroup_with_gate(): lax.all_to_all(blocks, 'qb', split_axis=1, concat_axis=1, tiled=True)  11.1 us
    all_to_all x2, starting transfers between devices, regroup_with_gate(): lax.all_to_all(jnp.stack(jnp.split(blocks, lax.axis_size('qa'), axis=1)),...  9.08 us
    unnamed x14, other arithmetic  8.87 us
    dot_general x8, matrix products, apply_gate(): lax.dot_general(values, stacked, (((1,), (1,)), ((), ())), precision=lax....  8.77 us
    dot_general x8, matrix products, apply_gate(): lax.dot_general(stacked, values, (((1,), (2,)), ((), ())), precision=lax....  7.85 us
    dot_general x8, matrix products, apply_gate(): lax.dot_general(stacked, values, (((1,), (1,)), ((), ())), precision=lax....  7.84 us
  transfers between devices with their start and end apart: 3, of which 3 were waited for; matrix products, arithmetic and copies ran while one was open for 3% of the time, Pallas kernels for 0%

profile of v1, /device:TPU:32, one launch (start us, length us, event | category | flops | bytes accessed | tf_op | source)
XLA Modules:
  0.0 114.1 jit_solution(13731846556905242782)
XLA Ops:
  0.0 2.2 %slice_bitcast_fusion.3 = (f32[128,128]{1,0:T(8,128)S(1)}, f32[128,128]{1,0:T(8,128)S(1)}, f32[128,128]{1,0:T(8,128)S(1)}, f32[128,128]{1,0:T(8,128)S(1)}, f32[1...) fusion(f32[4,6,2,128,128]{4,3,2,1,0:T(8,128)} %param.6), kind=kLoop, calls=%fused_computation.280 | loop fusion | bytes 2490368 | tf_op jit(solution)/shard_map/squeeze | solution.py:10
  2.2 2.1 %slice_bitcast_fusion.21 = (f32[128,128]{1,0:T(8,128)}, f32[128,128]{1,0:T(8,128)}, f32[128,128]{1,0:T(8,128)}, f32[128,128]{1,0:T(8,128)S(1)}, f32[128,128]{1,0...) fusion(f32[4,6,2,128,128]{4,3,2,1,0:T(8,128)} %param.6), kind=kLoop, calls=%fused_computation.298 | loop fusion | bytes 2490368 | tf_op jit(solution)/shard_map/squeeze | solution.py:10
  4.8 1.9 %convolution_bitcast_fusion = f32[1024,256]{0,1:T(8,128)S(1)} fusion(f32[1024,128]{1,0:T(8,128)S(1)} %reshape_reshape.2, f32[128,128]{1,0:T(8,128)} %get-tuple-element.20, f32[128,128]{1,0:T(8,128)} %get-tuple-element.21), kind=kOutput, calls=%fused_computation | convolution fusion | flops 402685952 | bytes 1703936 | tf_op jit(solution)/shard_map/dot_general | solution.py:13
  6.6 0.9 reshape.1375
  8.4 1.0 pad_maximum_fusion.15
  9.3 1.0 fusion
  10.5 1.0 fusion.3
  11.8 1.0 fusion.6
  12.9 1.0 fusion.9
  14.1 1.0 fusion.12
  15.5 0.7 fusion.159
  16.2 1.8 %multiply_add_fusion.1 = (f32[1,8,64,128]{3,2,1,0:T(8,128)S(1)}, f32[1,8,64,128]{3,2,1,0:T(8,128)S(1)}) fusion(f32[1,8,64,128]{3,2,1,0:T(8,128)S(1)} %add.638, f32[1,8,64,128]{3,2,1,0:T(8,128)S(1)} %sub.368, f32[64,128]{1,0:T(8,128)S(1)} %bitcast.643, f32[8,64]{1,0:T(8,128)S(1)} %copy.59, f32[]{:T(128)} %bitcast.105), kind=kLoop, calls=%fused_computation.198 | loop fusion | flops 524288 | bytes 1083396 | tf_op jit(solution)/shard_map/add | solution.py:44
  18.0 0.6 fusion.117
  18.7 0.6 fusion.120
  19.3 0.6 fusion.123
  21.9 0.6 fusion.114
  23.1 5.3 %all-to-all-start = ((f32[8,2,1,64,128]{4,3,1,2,0:T(8,128)}), f32[8,2,1,64,128]{4,3,1,2,0:T(8,128)S(1)}, u32[]{:S(2)}, u32[]{:S(2)}) async-start(f32[8,2,1,64,128]{4,3,1,2,0:T(8,128)} %fusion.136), calls=%async_computation | async-start | bytes 1048576 | tf_op jit(solution)/shard_map/all_to_all | solution.py:61
  28.8 9.7 %all-to-all-done = f32[8,2,1,64,128]{4,3,1,2,0:T(8,128)S(1)} async-done(((f32[8,2,1,64,128]{4,3,1,2,0:T(8,128)}), f32[8,2,1,64,128]{4,3,1,2,0:T(8,128)S(1)}, u32[]{:S(2)}, u32[]{:S(2)}) %all-to-all-start) | async-done | bytes 524320 | tf_op jit(solution)/shard_map/all_to_all | solution.py:61
  38.6 1.0 fusion.160
  39.6 1.0 fusion.15
  40.8 1.0 fusion.18
  41.9 1.0 fusion.21
  43.0 1.0 fusion.24
  44.1 1.0 fusion.27
  45.3 1.7 %fusion.78 = (f32[1,32,16,128]{3,2,0,1:T(8,128)S(1)}, f32[1,32,16,128]{3,2,0,1:T(8,128)S(1)}) fusion(f32[1,32,16,128]{3,2,1,0:T(8,128)S(1)} %add.663, f32[1,32,16,128]{3,2,1,0:T(8,128)S(1)} %sub.381, f32[16,128]{1,0:T(8,128)S(1)} %bitcast.646, f32[32,16]{1,0:T(8,128)S(1)} %copy.69, f32[]{:T(128)} %bitcast.148), kind=kLoop, calls=%fused_computation.183 | loop fusion | flops 524288 | bytes 1058820 | tf_op jit(solution)/shard_map/sub | solution.py:44
  47.0 0.8 pad_maximum_fusion
  47.8 11.1 %all-to-all-start.1 = ((f32[2,32,16,128]{3,2,0,1:T(8,128)}), f32[2,32,16,128]{3,2,0,1:T(8,128)S(1)}, u32[]{:S(2)}, u32[]{:S(2)}) async-start(f32[2,32,16,128]{3,2,0,1:T(8,128)} %pad_maximum_fusion), calls=%async_computation.1 | async-start | bytes 1048576 | tf_op jit(solution)/shard_map/all_to_all | solution.py:70
  59.1 1.6 %fusion.80 = (f32[256,256]{1,0:T(8,128)S(1)}, f32[256,256]{1,0:T(8,128)S(1)}) fusion(f32[256]{0:T(256)S(1)} %bitcast.649, f32[256]{0:T(256)S(1)} %bitcast.648, f32[]{:T(128)} %bitcast.227), kind=kLoop, calls=%fused_computation.188 | loop fusion | flops 131072 | bytes 526340 | tf_op jit(solution)/shard_map/sin | solution.py:43
  61.4 1.2 %slice_bitcast_fusion.41 = (f32[128,128]{1,0:T(8,128)S(1)}, f32[128,128]{1,0:T(8,128)S(1)}, f32[128,128]{1,0:T(8,128)S(1)}, f32[128,128]{1,0:T(8,128)S(1)}, f32[...) fusion(f32[4,6,2,128,128]{4,3,2,1,0:T(8,128)} %param.6), kind=kLoop, calls=%fused_computation.318 | loop fusion | bytes 1310720 | tf_op jit(solution)/shard_map/squeeze | solution.py:10
  62.6 15.6 %all-to-all-done.1 = f32[2,32,16,128]{3,2,0,1:T(8,128)S(1)} async-done(((f32[2,32,16,128]{3,2,0,1:T(8,128)}), f32[2,32,16,128]{3,2,0,1:T(8,128)S(1)}, u32[]{:S(2)}, u32[]{:S(2)}) %all-to-all-start.1) | async-done | bytes 524320 | tf_op jit(solution)/shard_map/all_to_all | solution.py:70
  78.2 1.0 fusion.161
  79.3 1.0 fusion.30
  80.4 1.0 fusion.33
  81.5 1.0 fusion.36
  82.6 1.0 fusion.39
  83.7 1.0 fusion.42
  84.9 1.9 %multiply_add_fusion = (f32[1,8,64,128]{3,2,1,0:T(8,128)S(1)}, f32[1,8,64,128]{3,2,1,0:T(8,128)S(1)}) fusion(f32[1,8,64,128]{3,2,1,0:T(8,128)S(1)} %add.688, f32[1,8,64,128]{3,2,1,0:T(8,128)S(1)} %sub.394, f32[64,128]{1,0:T(8,128)S(1)} %bitcast.642, f32[8,64]{1,0:T(8,128)S(1)} %copy.76, f32[]{:T(128)} %bitcast.184), kind=kLoop, calls=%fused_computation.190 | loop fusion | flops 524288 | bytes 1083396 | tf_op jit(solution)/shard_map/add | solution.py:44
  86.8 0.6 fusion.96
  90.6 0.6 fusion.93
  91.8 3.8 %all-to-all-start.2 = ((f32[8,2,1,64,128]{4,3,1,2,0:T(8,128)}), f32[8,2,1,64,128]{4,3,1,2,0:T(8,128)S(1)}, u32[]{:S(2)}, u32[]{:S(2)}) async-start(f32[8,2,1,64,128]{4,3,1,2,0:T(8,128)} %fusion.134), calls=%async_computation.2 | async-start | bytes 1048576 | tf_op jit(solution)/shard_map/all_to_all | solution.py:61
  95.7 9.3 %all-to-all-done.2 = f32[8,2,1,64,128]{4,3,1,2,0:T(8,128)S(1)} async-done(((f32[8,2,1,64,128]{4,3,1,2,0:T(8,128)}), f32[8,2,1,64,128]{4,3,1,2,0:T(8,128)S(1)}, u32[]{:S(2)}, u32[]{:S(2)}) %all-to-all-start.2) | async-done | bytes 524320 | tf_op jit(solution)/shard_map/all_to_all | solution.py:61
  105.1 1.0 fusion.162
  106.1 1.0 fusion.45
  107.3 1.0 fusion.48
  108.4 1.0 fusion.51
  109.5 1.0 fusion.54
  110.6 1.0 fusion.57
  112.9 1.3 %maximum_bitcast_fusion.40 = f32[2,65536]{1,0:T(2,128)} fusion(f32[1,1,65536]{2,0,1:T(1,128)S(1)} %get-tuple-element.57, f32[1,1,65536]{2,0,1:T(1,128)S(1)} %get-tuple-element.56), kind=kLoop, calls=%fused_computation.110 | loop fusion | flops 131072 | bytes 1048576 | tf_op jit(solution)/shard_map/reshape | solution.py:93
  (133 shorter events, 12.9 us)
Async XLA Ops:
  0.0 4.3 %copy-start = (f32[2,65536]{1,0:T(2,128)S(1)}, f32[2,65536]{1,0:T(2,128)}, u32[]{:S(2)}) copy-start(f32[2,65536]{1,0:T(2,128)} %param.5) | copy-start | bytes 1572868
  10.3 1.4 %copy-start.7 = (f32[128,128]{1,0:T(8,128)S(1)}, f32[128,128]{1,0:T(8,128)}, u32[]{:S(2)}) copy-start(f32[128,128]{1,0:T(8,128)} %get-tuple-element.14) | copy-start | bytes 196612
  10.3 1.4 %copy-start.8 = (f32[128,128]{1,0:T(8,128)S(1)}, f32[128,128]{1,0:T(8,128)}, u32[]{:S(2)}) copy-start(f32[128,128]{1,0:T(8,128)} %get-tuple-element.15) | copy-start | bytes 196612
  10.3 1.4 %copy-start.9 = (f32[128,128]{1,0:T(8,128)S(1)}, f32[128,128]{1,0:T(8,128)}, u32[]{:S(2)}) copy-start(f32[128,128]{1,0:T(8,128)} %get-tuple-element.18) | copy-start | bytes 196612
  10.4 1.4 %copy-start.10 = (f32[128,128]{1,0:T(8,128)S(1)}, f32[128,128]{1,0:T(8,128)}, u32[]{:S(2)}) copy-start(f32[128,128]{1,0:T(8,128)} %get-tuple-element.19) | copy-start | bytes 196612
  11.5 1.3 %copy-start.3 = (f32[128,128]{1,0:T(8,128)S(1)}, f32[128,128]{1,0:T(8,128)}, u32[]{:S(2)}) copy-start(f32[128,128]{1,0:T(8,128)} %get-tuple-element.26) | copy-start | bytes 196612
  11.5 1.3 %copy-start.4 = (f32[128,128]{1,0:T(8,128)S(1)}, f32[128,128]{1,0:T(8,128)}, u32[]{:S(2)}) copy-start(f32[128,128]{1,0:T(8,128)} %get-tuple-element.27) | copy-start | bytes 196612
  11.5 1.3 %copy-start.5 = (f32[128,128]{1,0:T(8,128)S(1)}, f32[128,128]{1,0:T(8,128)}, u32[]{:S(2)}) copy-start(f32[128,128]{1,0:T(8,128)} %get-tuple-element.28) | copy-start | bytes 196612
  11.5 1.3 %copy-start.6 = (f32[128,128]{1,0:T(8,128)S(1)}, f32[128,128]{1,0:T(8,128)}, u32[]{:S(2)}) copy-start(f32[128,128]{1,0:T(8,128)} %get-tuple-element.29) | copy-start | bytes 196612
  13.9 1.3 %copy-start.12 = (f32[4,256]{1,0:T(4,128)S(1)}, f32[4,256]{1,0:T(4,128)}, u32[]{:S(2)}) copy-start(f32[4,256]{1,0:T(4,128)} %param.8) | copy-start | bytes 12292
  14.0 1.5 %copy-start.13 = (f32[4,256]{1,0:T(4,128)S(1)}, f32[4,256]{1,0:T(4,128)}, u32[]{:S(2)}) copy-start(f32[4,256]{1,0:T(4,128)} %param.7) | copy-start | bytes 12292
  14.0 1.5 %copy-start.11 = (f32[4,1,1]{0,2,1:T(1,128)S(1)}, f32[4,1,1]{0,2,1:T(1,128)}, u32[]{:S(2)}) copy-start(f32[4,1,1]{0,2,1:T(1,128)} %param.9) | copy-start | bytes 52
  18.0 10.7 %copy-start.1 = (f32[128,128]{1,0:T(8,128)S(1)}, f32[128,128]{1,0:T(8,128)}, u32[]{:S(2)}) copy-start(f32[128,128]{1,0:T(8,128)} %get-tuple-element.32) | copy-start | bytes 196612
  18.0 10.7 %copy-start.2 = (f32[128,128]{1,0:T(8,128)S(1)}, f32[128,128]{1,0:T(8,128)}, u32[]{:S(2)}) copy-start(f32[128,128]{1,0:T(8,128)} %get-tuple-element.33) | copy-start | bytes 196612
  23.1 15.4 %all-to-all-start = ((f32[8,2,1,64,128]{4,3,1,2,0:T(8,128)}), f32[8,2,1,64,128]{4,3,1,2,0:T(8,128)S(1)}, u32[]{:S(2)}, u32[]{:S(2)}) async-start(f32[8,2,1,64,128]{4,3,1,2,0:T(8,128)} %fusion.136), calls=%async_computation | async-start | bytes 1048576 | tf_op jit(solution)/shard_map/all_to_all | solution.py:61
  47.8 30.3 %all-to-all-start.1 = ((f32[2,32,16,128]{3,2,0,1:T(8,128)}), f32[2,32,16,128]{3,2,0,1:T(8,128)S(1)}, u32[]{:S(2)}, u32[]{:S(2)}) async-start(f32[2,32,16,128]{3,2,0,1:T(8,128)} %pad_maximum_fusion), calls=%async_computation.1 | async-start | bytes 1048576 | tf_op jit(solution)/shard_map/all_to_all | solution.py:70
  91.8 13.2 %all-to-all-start.2 = ((f32[8,2,1,64,128]{4,3,1,2,0:T(8,128)}), f32[8,2,1,64,128]{4,3,1,2,0:T(8,128)S(1)}, u32[]{:S(2)}, u32[]{:S(2)}) async-start(f32[8,2,1,64,128]{4,3,1,2,0:T(8,128)} %fusion.134), calls=%async_computation.2 | async-start | bytes 1048576 | tf_op jit(solution)/shard_map/all_to_all | solution.py:61
